TPU v7x, 32 devices: a whole 2x2x4 slice. The times are simulated.
32 devices in a mesh: tm: 8 (over z, x), wall: 4 (over y, core).
Axes of the slice: x: 2, y: 2, z: 4, core: 2. Of those that a mesh axis runs over, the one named last changes fastest.
Arguments:
- start_state: float32 [8, 3, 384, 512], P('tm', None, 'wall'), may hold values from -6 to 6
- end_state: float32 [8, 3, 384, 512], P('tm', None, None, 'wall'), may hold values from -6 to 6
- coupling: float32 [8, 3, 384, 512], P('tm', None, None, 'wall'), may hold values from 0.5 to 1.5
- inverse_ops: float32 [8, 384, 384], P('wall')
- mirror_rows: int32 [384], replicated, may hold values from 0 to 383, as said below
- slab_steps: int32 [8], P('tm'), may hold values from 1 to 8, as said below
Outputs:
- gradient: float32 [8, 3, 384, 512], P('tm', None, 'wall')
Inputs may be any that keep to these rules, and one draw needn't show every extreme that they name: mirror_rows is an involution that maps each row of block b = y // 96 to a row of block 3 - b. `slab_steps`: some slab takes 8 steps.
All inputs are finite; a program needn't handle non-finite values.
Results may differ from a plain program's by a relative error of at most 0.00028.
Values sent between devices are 32-bit elements; how exact they have to be, the bound alone decides.
No kernel may reach another device: no remote copies, remote signals or barrier semaphores. Data moves between devices by JAX's collectives and lax.ppermute only.
A program may use at most 64 MiB of HBM per device.

v0:
```python
import functools

import jax
import jax.numpy as jnp
from jax import lax
from jax.experimental import pallas as pl
from jax.experimental.pallas import tpu as pltpu
from jax.sharding import PartitionSpec as P

STEPS_MAX = 8
LANES = 128
HALF = LANES // 2


def return_order(count):
    return [*range(count // 2, count), *reversed(range(count // 2))]


def unorder(order, parts):
    return [parts[order.index(step)] for step in range(len(order))]


def split(values):
    high = values.astype(jnp.bfloat16)
    low = (values - high.astype(jnp.float32)).astype(jnp.bfloat16)
    return high, low


def swap_halves(values):
    return pltpu.roll(values, HALF, 1)


def left_half(shape):
    return lax.broadcasted_iota(jnp.int32, shape, 1) < HALF


def to_groups(first, second):
    left = left_half(first.shape)
    return jnp.where(left, first, swap_halves(second)), jnp.where(left, swap_halves(first), second)


def mirror_block(pieces, mirror_ref, block, rows, count):
    partner = count - 1 - block
    target = mirror_ref[block] - partner * rows
    lane = lax.broadcasted_iota(jnp.int32, (rows, rows), 0)
    one_hot = (lane == target).astype(jnp.bfloat16)
    values = jnp.concatenate(pieces, axis=1)
    high, low = split(values)
    return jnp.dot(
        jnp.concatenate([one_hot, one_hot], axis=1),
        jnp.concatenate([high, low], axis=0),
        preferred_element_type=jnp.float32,
    )


def prepare_kernel(count, rows, wall_ref, mirror_ref, end_ref, coupling_ref, ops_ref, ops_out, gains, base, *sends):
    wall = wall_ref[0]
    ny = ops_ref.shape[1]
    left = left_half((ny, LANES))
    for group in range(2):
        high, low = split(ops_ref[group])
        ops_out[group, :, 0:ny] = high
        ops_out[group, :, ny : 2 * ny] = high
        ops_out[group, :, 2 * ny : 3 * ny] = low
    gains[0, :, :LANES], gains[1, :, :LANES] = to_groups(coupling_ref[0], coupling_ref[1])
    gains[0, :, LANES:] = jnp.where(left, coupling_ref[2], 0.0)
    gains[1, :, LANES:] = jnp.where(left, 0.0, coupling_ref[2])
    base[0, :, :LANES], base[1, :, :LANES] = to_groups(end_ref[0], end_ref[1])
    base[0, :, LANES:] = end_ref[2]
    base[1, :, LANES:] = end_ref[2]
    for step in range(count):
        source = count - 1 - (wall ^ step)
        at = pl.ds(pl.multiple_of(source * rows, 8), rows)
        moved = mirror_block([end_ref[c, at, :] for c in range(3)], mirror_ref, source, rows, count)
        for c, sign in enumerate((1.0, -1.0, 1.0)):
            sends[step][c] = sign * moved[:, c * LANES : (c + 1) * LANES]


def adjoint_kernel(count, rows, wall_ref, steps_ref, mirror_ref, ops_ref, gains, base, *rest):
    pieces, outs = rest[:count], rest[count : 2 * count]
    scaled, state = rest[2 * count : 2 * count + 2], rest[2 * count + 2 :]
    wall = wall_ref[0]
    ny = base.shape[1]
    for step in range(count):
        block = wall ^ step
        partner = count - 1 - block
        at = pl.ds(pl.multiple_of(partner * rows, 8), rows)
        moved = mirror_block([pieces[step][c] for c in range(3)], mirror_ref, block, rows, count)
        pair = to_groups(moved[:, :LANES], -moved[:, LANES : 2 * LANES])
        for group in range(2):
            state[group][at, :LANES] = base[group, at, :LANES] - pair[group]
            state[group][at, LANES:] = base[group, at, LANES:] - moved[:, 2 * LANES :]

    def scale(group):
        high, low = split(gains[group] * state[group][...])
        scaled[group][0:ny] = high
        scaled[group][ny : 2 * ny] = low
        scaled[group][2 * ny : 3 * ny] = high

    def multiply(group):
        for at in (pl.ds(0, ny // 2), pl.ds(ny // 2, ny // 2)):
            state[group][at, :] = jnp.dot(ops_ref[group, at, :], scaled[group][...], preferred_element_type=jnp.float32)

    def advance(_, carry):
        scale(1)
        multiply(0)
        scale(0)
        multiply(1)
        return carry

    def advance_most(_, carry):
        for _ in range(STEPS_MAX):
            advance(0, 0)
        return carry

    steps = jnp.minimum(steps_ref[0], STEPS_MAX)
    scale(0)
    lax.fori_loop(0, steps // STEPS_MAX, advance_most, 0)
    lax.fori_loop(0, steps % STEPS_MAX, advance, 0)
    left = left_half((rows, LANES))
    for step in range(count):
        at = pl.ds(pl.multiple_of((wall ^ step) * rows, 8), rows)
        outs[step][0], outs[step][1] = to_groups(state[0][at, :LANES], state[1][at, :LANES])
        outs[step][2] = jnp.where(left, state[0][at, LANES:], state[1][at, LANES:])


def offset_kernel(count, wall_ref, start_ref, *rest):
    parts, out_ref = rest[:-1][::-1], rest[-1]
    wall = wall_ref[0]
    for step, part in enumerate(parts):
        at = pl.ds(pl.multiple_of((wall ^ step) * LANES, LANES), LANES)
        out_ref[:, :, at] = part[...] - start_ref[:, :, at]


def combine_kernel(count, wall_ref, offset_ref, *rest):
    parts, out_ref, held, sems = unorder(return_order(count), rest[:count]), *rest[count:]
    wall = wall_ref[0]
    copies = []
    for c in range(3):
        for step, part in enumerate(parts):
            at = pl.ds(pl.multiple_of((wall ^ step) * LANES, LANES), LANES)
            held[c, :, at] = part[c] - offset_ref[c, :, at]
        copies.append(pltpu.make_async_copy(held.at[c], out_ref.at[c], sems.at[c]))
        copies[-1].start()
    for copy in copies:
        copy.wait()


def send(part, steps, flip, shape):
    slabs, count = shape
    pairs = [(t * count + w, (t + steps) % slabs * count + (w ^ flip)) for t in range(slabs) for w in range(count)]
    return lax.ppermute(part, ("tm", "wall"), pairs)


def on_device(shape, start_state, end_state, coupling, inverse_ops, mirror_rows, slab_steps):
    slabs, count = shape
    rows = start_state.shape[2]
    ny = end_state.shape[2]
    start, end, gain = start_state[0], end_state[0], coupling[0]
    wall = lax.axis_index("wall").astype(jnp.int32).reshape(1)
    mirror_blocks = mirror_rows.reshape(count, 1, rows)
    smem = pl.BlockSpec(memory_space=pltpu.SMEM)
    vmem = pl.BlockSpec(memory_space=pltpu.VMEM)
    part = jax.ShapeDtypeStruct((3, rows, LANES), jnp.float32)
    wide = jax.ShapeDtypeStruct((2, ny, 2 * LANES), jnp.float32)
    limit = pltpu.CompilerParams(vmem_limit_bytes=24 << 20)

    outgoing = [
        lax.dynamic_slice(start, (0, 0, (wall[0] ^ step) * LANES), (3, rows, LANES)) for step in range(count)
    ]
    incoming = [send(part, -1, step, shape) for step, part in enumerate(outgoing)]

    inverse_ops, incoming[:2] = lax.optimization_barrier((inverse_ops, incoming[:2]))
    ops, gains, base, *mirrored = pl.pallas_call(
        functools.partial(prepare_kernel, count, rows),
        out_shape=[jax.ShapeDtypeStruct((2, ny, 3 * ny), jnp.bfloat16), wide, wide] + [part] * count,
        in_specs=[smem] + [vmem] * 4,
        out_specs=[vmem] * (3 + count),
        compiler_params=limit,
        cost_estimate=pl.CostEstimate(flops=10**8, bytes_accessed=4 << 20, transcendentals=0),
        name="prepare",
    )(wall, mirror_blocks, end, gain, inverse_ops)

    mirrored = mirrored[:1] + [send(part, 1, i, shape) for i, part in enumerate(mirrored) if i]
    mirrored[0], mirrored[-1] = lax.optimization_barrier((mirrored[0], mirrored[-1]))
    mirrored[0] = send(mirrored[0], 1, 0, shape)

    adjoint = pl.pallas_call(
        functools.partial(adjoint_kernel, count, rows),
        out_shape=[part] * count,
        in_specs=[smem, smem] + [vmem] * (4 + count),
        out_specs=[vmem] * count,
        scratch_shapes=[pltpu.VMEM((3 * ny, 2 * LANES), jnp.bfloat16)] * 2
        + [pltpu.VMEM((ny, 2 * LANES), jnp.float32)] * 2,
        compiler_params=limit,
        cost_estimate=pl.CostEstimate(flops=4 * 10**9, bytes_accessed=4 << 20, transcendentals=0),
        name="adjoint",
    )(wall, slab_steps, mirror_blocks, ops, gains, base, *incoming)
    returned = [adjoint[0]] + [send(adjoint[step], 0, step, shape) for step in range(1, count)]

    offset = pl.pallas_call(
        functools.partial(offset_kernel, count),
        out_shape=jax.ShapeDtypeStruct(start.shape, jnp.float32),
        in_specs=[smem, vmem] + [vmem] * count,
        out_specs=vmem,
        compiler_params=limit,
        cost_estimate=pl.CostEstimate(flops=10**6, bytes_accessed=40 << 20, transcendentals=0),
        name="offset",
    )(wall, start, *mirrored[::-1])
    gradient = pl.pallas_call(
        functools.partial(combine_kernel, count),
        out_shape=jax.ShapeDtypeStruct(start.shape, jnp.float32),
        in_specs=[smem, vmem] + [vmem] * count,
        out_specs=pl.BlockSpec(memory_space=pl.ANY),
        scratch_shapes=[pltpu.VMEM(start.shape, jnp.float32), pltpu.SemaphoreType.DMA((3,))],
        compiler_params=limit,
        cost_estimate=pl.CostEstimate(flops=10**6, bytes_accessed=3 << 20, transcendentals=0),
        name="combine",
    )(wall, offset, *[returned[step] for step in return_order(count)])
    return gradient[None]


def solution(mesh):
    in_specs = (
        P("tm", None, "wall", None),
        P("tm", None, None, "wall"),
        P("tm", None, None, "wall"),
        P("wall", None, None),
        P(),
        P("tm"),
    )
    out_specs = P("tm", None, "wall", None)
    shape = (mesh.shape["tm"], mesh.shape["wall"])
    return jax.shard_map(
        functools.partial(on_device, shape),
        mesh=mesh,
        in_specs=in_specs,
        out_specs=out_specs,
        check_vma=False,
    )
```

profile of v0, /device:TPU:0, one launch (start us, length us, event | category | flops | bytes accessed | tf_op | source)
XLA Modules:
  0.0 36.4 jit_solution(15868155752073468791)
XLA Ops:
  0.0 0.0 copy-start.1
  0.0 1.3 %dynamic-slice_bitcast_fusion = (f32[3,96,128]{2,1,0:T(8,128)S(1)}, f32[3,96,128]{2,1,0:T(8,128)S(1)}, f32[3,96,128]{2,1,0:T(8,128)S(1)}, f32[3,96,128]{2,1,0:T(8,128)S(1)}) fusion(f32[1,3,96,512]{3,2,1,0:T(8,128)} %param.6, s32[]{:T(128)S(6)} %select_n.15, s32[]{:T(128)S(6)} %select_n.13, s32[]{:T(128)S(6)} %select_n.12, s32[]{:T(128)S(6)} %select_n.14), kind=kLoop, calls=%fused_computation | loop fusion | bytes 1179664 | tf_op jit(solution)/shard_map/dynamic_slice | solution.py:169
  1.3 6.0 %collective-permute-start = (f32[3,96,128]{2,1,0:T(8,128)S(1)}, f32[3,96,128]{2,1,0:T(8,128)S(1)}, u32[]{:S(2)}, u32[]{:S(2)}) collective-permute-start(f32[3,96,128]{2,1,0:T(8,128)S(1)} %get-tuple-element.39), channel_id=1, source_target_pairs={{0,28},{1,29},{2,30},{3,31},{4,0},{5,1},{6,2},{7,3},{8,4},{9,5},{1... | collective-permute-start | bytes 442376 | tf_op jit(solution)/shard_map/ppermute | solution.py:152
  7.3 0.0 collective-permute-start.1
  7.3 2.0 %collective-permute-start.6 = (f32[3,96,128]{2,1,0:T(8,128)S(1)}, f32[3,96,128]{2,1,0:T(8,128)S(1)}, u32[]{:S(2)}, u32[]{:S(2)}) collective-permute-start(f32[3,96,128]{2,1,0:T(8,128)S(1)} %get-tuple-element.40), channel_id=1, source_target_pairs={{0,30},{1,31},{2,28},{3,29},{4,2},{5,3},{6,0},{7,1},{8,6},{9,7},{1... | collective-permute-start | bytes 442376 | tf_op jit(solution)/shard_map/ppermute | solution.py:152
  9.3 0.8 %collective-permute-start.7 = (f32[3,96,128]{2,1,0:T(8,128)S(1)}, f32[3,96,128]{2,1,0:T(8,128)S(1)}, u32[]{:S(2)}, u32[]{:S(2)}) collective-permute-start(f32[3,96,128]{2,1,0:T(8,128)S(1)} %get-tuple-element.37), channel_id=1, source_target_pairs={{0,31},{1,30},{2,29},{3,28},{4,3},{5,2},{6,1},{7,0},{8,7},{9,6},{1... | collective-permute-start | bytes 442376 | tf_op jit(solution)/shard_map/ppermute | solution.py:152
  10.1 0.8 %reshape.11.mirror_ref = s32[4,1,96]{2,1,0:T(1,128)S(1)} reshape(s32[384]{0:T(512)} %param.10) | data formatting | bytes 3072 | tf_op jit(solution)/shard_map/reshape | solution.py:161
  11.5 0.1 collective-permute-done.rest_0_
  11.6 3.2 %collective-permute-done.1.rest_1_ = f32[3,96,128]{2,1,0:T(8,128)S(1)} collective-permute-done((f32[3,96,128]{2,1,0:T(8,128)S(1)}, f32[3,96,128]{2,1,0:T(8,128)S(1)}, u32[]{:S(2)}, u32[]{:S(2)}) %collective-permute-start.1) | collective-permute-done | bytes 147488 | tf_op jit(solution)/shard_map/ppermute | solution.py:152
  14.7 0.0 copy-done.1
  14.7 0.0 copy-start.2
  14.7 1.1 %copy-done.2 = f32[1,3,384,128]{3,2,1,0:T(8,128)S(1)} copy-done((f32[1,3,384,128]{3,2,1,0:T(8,128)S(1)}, f32[1,3,384,128]{3,2,1,0:T(8,128)}, u32[]{:S(2)}) %copy-start.2) | copy-done | bytes 589848
  15.8 0.0 copy-start.3
  15.8 1.1 %copy-done.3 = f32[1,3,384,128]{3,2,1,0:T(8,128)S(1)} copy-done((f32[1,3,384,128]{3,2,1,0:T(8,128)S(1)}, f32[1,3,384,128]{3,2,1,0:T(8,128)}, u32[]{:S(2)}) %copy-start.3) | copy-done | bytes 589848
  16.8 0.7 %prepare.1 = (bf16[2,384,1152]{2,1,0:T(8,128)(2,1)S(1)}, f32[2,384,256]{2,1,0:T(8,128)S(1)}, f32[2,384,256]{2,1,0:T(8,128)S(1)}, f32[3,96,128]{2,1,0:T(8,128)S(1...) custom-call(s32[1]{0:T(128)} %bitcast.wall_ref, ...), custom_call_target="tpu_custom_call" | custom-call | flops 100000000 | bytes 4194304 | tf_op jit(solution)/shard_map/prepare/pallas_call | solution.py:174
  17.6 0.9 %collective-permute-start.2 = (f32[3,96,128]{2,1,0:T(8,128)S(1)}, f32[3,96,128]{2,1,0:T(8,128)S(1)}, u32[]{:S(2)}, u32[]{:S(2)}) collective-permute-start(f32[3,96,128]{2,1,0:T(8,128)S(1)} %get-tuple-element.23), channel_id=1, source_target_pairs={{0,7},{1,6},{2,5},{3,4},{4,11},{5,10},{6,9},{7,8},{8,15},{9,14},{1... | collective-permute-start | bytes 442376 | tf_op jit(solution)/shard_map/ppermute | solution.py:152
  18.5 0.5 %collective-permute-start.3 = (f32[3,96,128]{2,1,0:T(8,128)S(1)}, f32[3,96,128]{2,1,0:T(8,128)S(1)}, u32[]{:S(2)}, u32[]{:S(2)}) collective-permute-start(f32[3,96,128]{2,1,0:T(8,128)S(1)} %get-tuple-element.25), channel_id=1, source_target_pairs={{0,6},{1,7},{2,4},{3,5},{4,10},{5,11},{6,8},{7,9},{8,14},{9,15},{1... | collective-permute-start | bytes 442376 | tf_op jit(solution)/shard_map/ppermute | solution.py:152
  19.0 0.4 %collective-permute-start.4 = (f32[3,96,128]{2,1,0:T(8,128)S(1)}, f32[3,96,128]{2,1,0:T(8,128)S(1)}, u32[]{:S(2)}, u32[]{:S(2)}) collective-permute-start(f32[3,96,128]{2,1,0:T(8,128)S(1)} %get-tuple-element.26), channel_id=1, source_target_pairs={{0,5},{1,4},{2,7},{3,6},{4,9},{5,8},{6,11},{7,10},{8,13},{9,12},{1... | collective-permute-start | bytes 442376 | tf_op jit(solution)/shard_map/ppermute | solution.py:152
  19.3 0.0 collective-permute-done.6.rest_2_
  19.3 1.1 %collective-permute-done.7.rest_3_ = f32[3,96,128]{2,1,0:T(8,128)S(1)} collective-permute-done((f32[3,96,128]{2,1,0:T(8,128)S(1)}, f32[3,96,128]{2,1,0:T(8,128)S(1)}, u32[]{:S(2)}, u32[]{:S(2)}) %collective-permute-start.7) | collective-permute-done | bytes 147488 | tf_op jit(solution)/shard_map/ppermute | solution.py:152
  20.5 0.0 copy-start
  20.5 2.1 %adjoint.1 = (f32[3,96,128]{2,1,0:T(8,128)S(1)}, f32[3,96,128]{2,1,0:T(8,128)S(1)}, f32[3,96,128]{2,1,0:T(8,128)S(1)}, f32[3,96,128]{2,1,0:T(8,128)S(1)}) custom-call(s32[1]{0:T(128)} %bitcast.wall_ref, s32[1]{0:T(128)S(6)} %copy.7.steps_ref, s32[4,1,96]{2,1,0:T(1,128)S(1)} %reshape.11.mirror_ref, bf16[2,384,1152]{2,1,0:T(8,128)(2,1)S(1)} %get-tuple-element.28.ops_ref, ...), custom_call_target="tpu_custom_call" | custom-call | flops 4000000000 | bytes 4194304 | tf_op jit(solution)/shard_map/adjoint/pallas_call | solution.py:188
  22.6 4.4 %collective-permute-done.2.rest_0_ = f32[3,96,128]{2,1,0:T(8,128)S(1)} collective-permute-done((f32[3,96,128]{2,1,0:T(8,128)S(1)}, f32[3,96,128]{2,1,0:T(8,128)S(1)}, u32[]{:S(2)}, u32[]{:S(2)}) %collective-permute-start.2) | collective-permute-done | bytes 147488 | tf_op jit(solution)/shard_map/ppermute | solution.py:152
  27.0 0.0 collective-permute-start.5
  27.0 1.4 %collective-permute-start.8 = (f32[3,96,128]{2,1,0:T(8,128)S(1)}, f32[3,96,128]{2,1,0:T(8,128)S(1)}, u32[]{:S(2)}, u32[]{:S(2)}) collective-permute-start(f32[3,96,128]{2,1,0:T(8,128)S(1)} %get-tuple-element.33), channel_id=1, source_target_pairs={{0,2},{1,3},{2,0},{3,1},{4,6},{5,7},{6,4},{7,5},{8,10},{9,11},{10,... | collective-permute-start | bytes 442376 | tf_op jit(solution)/shard_map/ppermute | solution.py:152
  28.5 0.0 collective-permute-start.9
  28.5 0.4 %collective-permute-done.3.rest_1_ = f32[3,96,128]{2,1,0:T(8,128)S(1)} collective-permute-done((f32[3,96,128]{2,1,0:T(8,128)S(1)}, f32[3,96,128]{2,1,0:T(8,128)S(1)}, u32[]{:S(2)}, u32[]{:S(2)}) %collective-permute-start.3) | collective-permute-done | bytes 147488 | tf_op jit(solution)/shard_map/ppermute | solution.py:152
  28.9 1.1 %collective-permute-start.10 = (f32[3,96,128]{2,1,0:T(8,128)S(1)}, f32[3,96,128]{2,1,0:T(8,128)S(1)}, u32[]{:S(2)}, u32[]{:S(2)}) collective-permute-start(f32[3,96,128]{2,1,0:T(8,128)S(1)} %get-tuple-element.35), channel_id=1, source_target_pairs={{0,1},{1,0},{2,3},{3,2},{4,5},{5,4},{6,7},{7,6},{8,9},{9,8},{10,11... | collective-permute-start | bytes 442376 | tf_op jit(solution)/shard_map/ppermute | solution.py:152
  30.0 2.2 %collective-permute-done.4.rest_2_ = f32[3,96,128]{2,1,0:T(8,128)S(1)} collective-permute-done((f32[3,96,128]{2,1,0:T(8,128)S(1)}, f32[3,96,128]{2,1,0:T(8,128)S(1)}, u32[]{:S(2)}, u32[]{:S(2)}) %collective-permute-start.4) | collective-permute-done | bytes 147488 | tf_op jit(solution)/shard_map/ppermute | solution.py:152
  32.3 3.2 %collective-permute-done.5.rest_3_ = f32[3,96,128]{2,1,0:T(8,128)S(1)} collective-permute-done((f32[3,96,128]{2,1,0:T(8,128)S(1)}, f32[3,96,128]{2,1,0:T(8,128)S(1)}, u32[]{:S(2)}, u32[]{:S(2)}) %collective-permute-start.5) | collective-permute-done | bytes 147488 | tf_op jit(solution)/shard_map/ppermute | solution.py:152
  35.4 0.0 copy-done
  35.4 0.1 offset.1.offset_ref
  35.5 0.0 collective-permute-done.8.rest_0_
  35.5 0.0 collective-permute-done.9.rest_1_
  35.5 0.0 collective-permute-done.10.rest_2_
  35.6 0.9 %combine.1 = f32[3,96,512]{2,1,0:T(8,128)} custom-call(s32[1]{0:T(128)} %bitcast.wall_ref, f32[3,96,512]{2,1,0:T(8,128)S(1)} %offset.1.offset_ref, f32[3,96,128]{2,1,0:T(8,128)S(1)} %collective-permute-done.8.rest_0_, f32[3,96,128]{2,1,0:T(8,128)S(1)} %collective-permute-done.9.rest_1_, f32[3,96,128]{2,1,0:T(8,128)S(1)} %collective-permute-done.10.rest_2_, ...), custom_call_target="tpu_custom_call" | custom-call | flops 1000000 | bytes 3145728 | tf_op jit(solution)/shard_map/combine/pallas_call | solution.py:210
Async XLA Ops:
  0.0 14.7 %copy-start.1 = (f32[2,384,384]{2,1,0:T(8,128)S(1)}, f32[2,384,384]{2,1,0:T(8,128)}, u32[]{:S(2)}) copy-start(f32[2,384,384]{2,1,0:T(8,128)} %ops_ref) | copy-start | bytes 3538948
  1.3 10.3 %collective-permute-start = (f32[3,96,128]{2,1,0:T(8,128)S(1)}, f32[3,96,128]{2,1,0:T(8,128)S(1)}, u32[]{:S(2)}, u32[]{:S(2)}) collective-permute-start(f32[3,96,128]{2,1,0:T(8,128)S(1)} %get-tuple-element.39), channel_id=1, source_target_pairs={{0,28},{1,29},{2,30},{3,31},{4,0},{5,1},{6,2},{7,3},{8,4},{9,5},{1... | collective-permute-start | bytes 442376 | tf_op jit(solution)/shard_map/ppermute | solution.py:152
  7.3 7.4 %collective-permute-start.1 = (f32[3,96,128]{2,1,0:T(8,128)S(1)}, f32[3,96,128]{2,1,0:T(8,128)S(1)}, u32[]{:S(2)}, u32[]{:S(2)}) collective-permute-start(f32[3,96,128]{2,1,0:T(8,128)S(1)} %get-tuple-element.38), channel_id=1, source_target_pairs={{0,29},{1,28},{2,31},{3,30},{4,1},{5,0},{6,3},{7,2},{8,5},{9,4},{1... | collective-permute-start | bytes 442376 | tf_op jit(solution)/shard_map/ppermute | solution.py:152
  7.3 12.0 %collective-permute-start.6 = (f32[3,96,128]{2,1,0:T(8,128)S(1)}, f32[3,96,128]{2,1,0:T(8,128)S(1)}, u32[]{:S(2)}, u32[]{:S(2)}) collective-permute-start(f32[3,96,128]{2,1,0:T(8,128)S(1)} %get-tuple-element.40), channel_id=1, source_target_pairs={{0,30},{1,31},{2,28},{3,29},{4,2},{5,3},{6,0},{7,1},{8,6},{9,7},{1... | collective-permute-start | bytes 442376 | tf_op jit(solution)/shard_map/ppermute | solution.py:152
  9.3 11.1 %collective-permute-start.7 = (f32[3,96,128]{2,1,0:T(8,128)S(1)}, f32[3,96,128]{2,1,0:T(8,128)S(1)}, u32[]{:S(2)}, u32[]{:S(2)}) collective-permute-start(f32[3,96,128]{2,1,0:T(8,128)S(1)} %get-tuple-element.37), channel_id=1, source_target_pairs={{0,31},{1,30},{2,29},{3,28},{4,3},{5,2},{6,1},{7,0},{8,7},{9,6},{1... | collective-permute-start | bytes 442376 | tf_op jit(solution)/shard_map/ppermute | solution.py:152
  14.7 1.1 %copy-start.2 = (f32[1,3,384,128]{3,2,1,0:T(8,128)S(1)}, f32[1,3,384,128]{3,2,1,0:T(8,128)}, u32[]{:S(2)}) copy-start(f32[1,3,384,128]{3,2,1,0:T(8,128)} %param.7) | copy-start | bytes 1769476
  15.8 1.1 %copy-start.3 = (f32[1,3,384,128]{3,2,1,0:T(8,128)S(1)}, f32[1,3,384,128]{3,2,1,0:T(8,128)}, u32[]{:S(2)}) copy-start(f32[1,3,384,128]{3,2,1,0:T(8,128)} %param.8) | copy-start | bytes 1769476
  17.6 9.4 %collective-permute-start.2 = (f32[3,96,128]{2,1,0:T(8,128)S(1)}, f32[3,96,128]{2,1,0:T(8,128)S(1)}, u32[]{:S(2)}, u32[]{:S(2)}) collective-permute-start(f32[3,96,128]{2,1,0:T(8,128)S(1)} %get-tuple-element.23), channel_id=1, source_target_pairs={{0,7},{1,6},{2,5},{3,4},{4,11},{5,10},{6,9},{7,8},{8,15},{9,14},{1... | collective-permute-start | bytes 442376 | tf_op jit(solution)/shard_map/ppermute | solution.py:152
  18.5 10.4 %collective-permute-start.3 = (f32[3,96,128]{2,1,0:T(8,128)S(1)}, f32[3,96,128]{2,1,0:T(8,128)S(1)}, u32[]{:S(2)}, u32[]{:S(2)}) collective-permute-start(f32[3,96,128]{2,1,0:T(8,128)S(1)} %get-tuple-element.25), channel_id=1, source_target_pairs={{0,6},{1,7},{2,4},{3,5},{4,10},{5,11},{6,8},{7,9},{8,14},{9,15},{1... | collective-permute-start | bytes 442376 | tf_op jit(solution)/shard_map/ppermute | solution.py:152
  19.0 13.3 %collective-permute-start.4 = (f32[3,96,128]{2,1,0:T(8,128)S(1)}, f32[3,96,128]{2,1,0:T(8,128)S(1)}, u32[]{:S(2)}, u32[]{:S(2)}) collective-permute-start(f32[3,96,128]{2,1,0:T(8,128)S(1)} %get-tuple-element.26), channel_id=1, source_target_pairs={{0,5},{1,4},{2,7},{3,6},{4,9},{5,8},{6,11},{7,10},{8,13},{9,12},{1... | collective-permute-start | bytes 442376 | tf_op jit(solution)/shard_map/ppermute | solution.py:152
  20.5 15.0 %copy-start = (f32[1,3,96,512]{3,2,1,0:T(8,128)S(1)}, f32[1,3,96,512]{3,2,1,0:T(8,128)}, u32[]{:S(2)}) copy-start(f32[1,3,96,512]{3,2,1,0:T(8,128)} %param.6) | copy-start | bytes 1769476
  27.0 8.4 %collective-permute-start.5 = (f32[3,96,128]{2,1,0:T(8,128)S(1)}, f32[3,96,128]{2,1,0:T(8,128)S(1)}, u32[]{:S(2)}, u32[]{:S(2)}) collective-permute-start(f32[3,96,128]{2,1,0:T(8,128)S(1)} %get-tuple-element.27), channel_id=1, source_target_pairs={{0,4},{1,5},{2,6},{3,7},{4,8},{5,9},{6,10},{7,11},{8,12},{9,13},{1... | collective-permute-start | bytes 442376 | tf_op jit(solution)/shard_map/ppermute | solution.py:152
  27.0 8.5 %collective-permute-start.8 = (f32[3,96,128]{2,1,0:T(8,128)S(1)}, f32[3,96,128]{2,1,0:T(8,128)S(1)}, u32[]{:S(2)}, u32[]{:S(2)}) collective-permute-start(f32[3,96,128]{2,1,0:T(8,128)S(1)} %get-tuple-element.33), channel_id=1, source_target_pairs={{0,2},{1,3},{2,0},{3,1},{4,6},{5,7},{6,4},{7,5},{8,10},{9,11},{10,... | collective-permute-start | bytes 442376 | tf_op jit(solution)/shard_map/ppermute | solution.py:152
  28.5 7.1 %collective-permute-start.9 = (f32[3,96,128]{2,1,0:T(8,128)S(1)}, f32[3,96,128]{2,1,0:T(8,128)S(1)}, u32[]{:S(2)}, u32[]{:S(2)}) collective-permute-start(f32[3,96,128]{2,1,0:T(8,128)S(1)} %get-tuple-element.34), channel_id=1, source_target_pairs={{0,3},{1,2},{2,1},{3,0},{4,7},{5,6},{6,5},{7,4},{8,11},{9,10},{10,... | collective-permute-start | bytes 442376 | tf_op jit(solution)/shard_map/ppermute | solution.py:152
  28.9 6.7 %collective-permute-start.10 = (f32[3,96,128]{2,1,0:T(8,128)S(1)}, f32[3,96,128]{2,1,0:T(8,128)S(1)}, u32[]{:S(2)}, u32[]{:S(2)}) collective-permute-start(f32[3,96,128]{2,1,0:T(8,128)S(1)} %get-tuple-element.35), channel_id=1, source_target_pairs={{0,1},{1,0},{2,3},{3,2},{4,5},{5,4},{6,7},{7,6},{8,9},{9,8},{10,11... | collective-permute-start | bytes 442376 | tf_op jit(solution)/shard_map/ppermute | solution.py:152
where the time goes:
time: 37 us; the launch traced here: 36.4 us
  waiting for transfers between devices  14.6 us (39%)
  starting transfers between devices  13.1 us (35%)
  local copies, waits for them, and re-layouts  4.17 us (11%)
  Pallas kernels  3.83 us (10%)
  between operations  0.71 us (2%)
    ppermute x11, waiting for transfers between devices, send(): return lax.ppermute(part, ('tm', 'wall'), pairs)  14.6 us
    ppermute x11, starting transfers between devices, send(): return lax.ppermute(part, ('tm', 'wall'), pairs)  13.1 us
    unnamed x8, local copies, waits for them, and re-layouts  2.14 us
    pallas_call x1, Pallas kernels, on_device(): pl.pallas_call(functools.partial(adjoint_kernel, count, rows), out_shape=...  2.13 us
    dynamic_slice x1, local copies, waits for them, and re-layouts, on_device(): lax.dynamic_slice(start, (0, 0, (wall[0] ^ step) * LANES), (3, rows, LANES))  1.27 us
    pallas_call x1, Pallas kernels, on_device(): pl.pallas_call(functools.partial(combine_kernel, count), out_shape=jax.Sh...  0.87 us
    reshape x1, local copies, waits for them, and re-layouts, on_device(): mirror_blocks = mirror_rows.reshape(count, 1, rows)  0.76 us
  transfers between devices with their start and end apart: 11, of which 6 were waited for; matrix products, arithmetic and copies ran while one was open for 2% of the time, Pallas kernels for 8%

commit v1 on v0

--- a/solution.py
+++ b/solution.py
@@ -181,6 +181,7 @@
         name="prepare",
     )(wall, mirror_blocks, end, gain, inverse_ops)
 
+    mirrored[1], incoming[2] = lax.optimization_barrier((mirrored[1], incoming[2]))
     mirrored = mirrored[:1] + [send(part, 1, i, shape) for i, part in enumerate(mirrored) if i]
     mirrored[0], mirrored[-1] = lax.optimization_barrier((mirrored[0], mirrored[-1]))
     mirrored[0] = send(mirrored[0], 1, 0, shape)

time: 37 us -> 36.7 us (level)
  no operation moved by 1% of the time
where the time goes in v1:
time: 36.7 us; the launch traced here: 36.4 us
  waiting for transfers between devices  14.6 us (40%)
  starting transfers between devices  13.1 us (36%)
  local copies, waits for them, and re-layouts  4.17 us (11%)
  Pallas kernels  3.83 us (10%)
  between operations  0.71 us (2%)
    ppermute x11, waiting for transfers between devices, send(): return lax.ppermute(part, ('tm', 'wall'), pairs)  14.6 us
    ppermute x11, starting transfers between devices, send(): return lax.ppermute(part, ('tm', 'wall'), pairs)  13.1 us
    unnamed x8, local copies, waits for them, and re-layouts  2.14 us
    pallas_call x1, Pallas kernels, on_device(): pl.pallas_call(functools.partial(adjoint_kernel, count, rows), out_shape=...  2.13 us
    dynamic_slice x1, local copies, waits for them, and re-layouts, on_device(): lax.dynamic_slice(start, (0, 0, (wall[0] ^ step) * LANES), (3, rows, LANES))  1.27 us
    pallas_call x1, Pallas kernels, on_device(): pl.pallas_call(functools.partial(combine_kernel, count), out_shape=jax.Sh...  0.87 us
    reshape x1, local copies, waits for them, and re-layouts, on_device(): mirror_blocks = mirror_rows.reshape(count, 1, rows)  0.76 us
  transfers between devices with their start and end apart: 11, of which 6 were waited for; matrix products, arithmetic and copies ran while one was open for 2% of the time, Pallas kernels for 8%

profile of v1, /device:TPU:0, one launch (start us, length us, event | category | flops | bytes accessed | tf_op | source)
XLA Modules:
  0.0 36.4 jit_solution(7293138582555062577)
XLA Ops:
  0.0 0.0 copy-start.1
  0.0 1.3 %dynamic-slice_bitcast_fusion = (f32[3,96,128]{2,1,0:T(8,128)S(1)}, f32[3,96,128]{2,1,0:T(8,128)S(1)}, f32[3,96,128]{2,1,0:T(8,128)S(1)}, f32[3,96,128]{2,1,0:T(8,128)S(1)}) fusion(f32[1,3,96,512]{3,2,1,0:T(8,128)} %param.6, s32[]{:T(128)S(6)} %select_n.15, s32[]{:T(128)S(6)} %select_n.13, s32[]{:T(128)S(6)} %select_n.12, s32[]{:T(128)S(6)} %select_n.14), kind=kLoop, calls=%fused_computation | loop fusion | bytes 1179664 | tf_op jit(solution)/shard_map/dynamic_slice | solution.py:169
  1.3 6.0 %collective-permute-start = (f32[3,96,128]{2,1,0:T(8,128)S(1)}, f32[3,96,128]{2,1,0:T(8,128)S(1)}, u32[]{:S(2)}, u32[]{:S(2)}) collective-permute-start(f32[3,96,128]{2,1,0:T(8,128)S(1)} %get-tuple-element.43), channel_id=1, source_target_pairs={{0,28},{1,29},{2,30},{3,31},{4,0},{5,1},{6,2},{7,3},{8,4},{9,5},{1... | collective-permute-start | bytes 442376 | tf_op jit(solution)/shard_map/ppermute | solution.py:152
  7.3 0.0 collective-permute-start.1
  7.3 2.0 %collective-permute-start.4 = (f32[3,96,128]{2,1,0:T(8,128)S(1)}, f32[3,96,128]{2,1,0:T(8,128)S(1)}, u32[]{:S(2)}, u32[]{:S(2)}) collective-permute-start(f32[3,96,128]{2,1,0:T(8,128)S(1)} %get-tuple-element.44), channel_id=1, source_target_pairs={{0,30},{1,31},{2,28},{3,29},{4,2},{5,3},{6,0},{7,1},{8,6},{9,7},{1... | collective-permute-start | bytes 442376 | tf_op jit(solution)/shard_map/ppermute | solution.py:152
  9.3 0.8 %collective-permute-start.7 = (f32[3,96,128]{2,1,0:T(8,128)S(1)}, f32[3,96,128]{2,1,0:T(8,128)S(1)}, u32[]{:S(2)}, u32[]{:S(2)}) collective-permute-start(f32[3,96,128]{2,1,0:T(8,128)S(1)} %get-tuple-element.41), channel_id=1, source_target_pairs={{0,31},{1,30},{2,29},{3,28},{4,3},{5,2},{6,1},{7,0},{8,7},{9,6},{1... | collective-permute-start | bytes 442376 | tf_op jit(solution)/shard_map/ppermute | solution.py:152
  10.1 0.8 %reshape.11.mirror_ref = s32[4,1,96]{2,1,0:T(1,128)S(1)} reshape(s32[384]{0:T(512)} %param.10) | data formatting | bytes 3072 | tf_op jit(solution)/shard_map/reshape | solution.py:161
  11.5 0.1 collective-permute-done.rest_0_
  11.6 3.2 %collective-permute-done.1.rest_1_ = f32[3,96,128]{2,1,0:T(8,128)S(1)} collective-permute-done((f32[3,96,128]{2,1,0:T(8,128)S(1)}, f32[3,96,128]{2,1,0:T(8,128)S(1)}, u32[]{:S(2)}, u32[]{:S(2)}) %collective-permute-start.1) | collective-permute-done | bytes 147488 | tf_op jit(solution)/shard_map/ppermute | solution.py:152
  14.7 0.0 copy-done.1
  14.7 0.0 copy-start.2
  14.7 1.1 %copy-done.2 = f32[1,3,384,128]{3,2,1,0:T(8,128)S(1)} copy-done((f32[1,3,384,128]{3,2,1,0:T(8,128)S(1)}, f32[1,3,384,128]{3,2,1,0:T(8,128)}, u32[]{:S(2)}) %copy-start.2) | copy-done | bytes 589848
  15.8 0.0 copy-start.3
  15.8 1.1 %copy-done.3 = f32[1,3,384,128]{3,2,1,0:T(8,128)S(1)} copy-done((f32[1,3,384,128]{3,2,1,0:T(8,128)S(1)}, f32[1,3,384,128]{3,2,1,0:T(8,128)}, u32[]{:S(2)}) %copy-start.3) | copy-done | bytes 589848
  16.8 0.7 %prepare.1 = (bf16[2,384,1152]{2,1,0:T(8,128)(2,1)S(1)}, f32[2,384,256]{2,1,0:T(8,128)S(1)}, f32[2,384,256]{2,1,0:T(8,128)S(1)}, f32[3,96,128]{2,1,0:T(8,128)S(1...) custom-call(s32[1]{0:T(128)} %bitcast.wall_ref, ...), custom_call_target="tpu_custom_call" | custom-call | flops 100000000 | bytes 4194304 | tf_op jit(solution)/shard_map/prepare/pallas_call | solution.py:174
  17.6 0.9 %collective-permute-start.2 = (f32[3,96,128]{2,1,0:T(8,128)S(1)}, f32[3,96,128]{2,1,0:T(8,128)S(1)}, u32[]{:S(2)}, u32[]{:S(2)}) collective-permute-start(f32[3,96,128]{2,1,0:T(8,128)S(1)} %get-tuple-element.25), channel_id=1, source_target_pairs={{0,7},{1,6},{2,5},{3,4},{4,11},{5,10},{6,9},{7,8},{8,15},{9,14},{1... | collective-permute-start | bytes 442376 | tf_op jit(solution)/shard_map/ppermute | solution.py:152
  18.5 0.5 %collective-permute-start.3 = (f32[3,96,128]{2,1,0:T(8,128)S(1)}, f32[3,96,128]{2,1,0:T(8,128)S(1)}, u32[]{:S(2)}, u32[]{:S(2)}) collective-permute-start(f32[3,96,128]{2,1,0:T(8,128)S(1)} %get-tuple-element.27), channel_id=1, source_target_pairs={{0,6},{1,7},{2,4},{3,5},{4,10},{5,11},{6,8},{7,9},{8,14},{9,15},{1... | collective-permute-start | bytes 442376 | tf_op jit(solution)/shard_map/ppermute | solution.py:152
  19.0 0.0 collective-permute-done.4.rest_2_
  19.0 0.4 %collective-permute-start.5 = (f32[3,96,128]{2,1,0:T(8,128)S(1)}, f32[3,96,128]{2,1,0:T(8,128)S(1)}, u32[]{:S(2)}, u32[]{:S(2)}) collective-permute-start(f32[3,96,128]{2,1,0:T(8,128)S(1)} %get-tuple-element.29), channel_id=1, source_target_pairs={{0,5},{1,4},{2,7},{3,6},{4,9},{5,8},{6,11},{7,10},{8,13},{9,12},{1... | collective-permute-start | bytes 442376 | tf_op jit(solution)/shard_map/ppermute | solution.py:152
  19.3 1.1 %collective-permute-done.7.rest_3_ = f32[3,96,128]{2,1,0:T(8,128)S(1)} collective-permute-done((f32[3,96,128]{2,1,0:T(8,128)S(1)}, f32[3,96,128]{2,1,0:T(8,128)S(1)}, u32[]{:S(2)}, u32[]{:S(2)}) %collective-permute-start.7) | collective-permute-done | bytes 147488 | tf_op jit(solution)/shard_map/ppermute | solution.py:152
  20.5 0.0 copy-start
  20.5 2.1 %adjoint.1 = (f32[3,96,128]{2,1,0:T(8,128)S(1)}, f32[3,96,128]{2,1,0:T(8,128)S(1)}, f32[3,96,128]{2,1,0:T(8,128)S(1)}, f32[3,96,128]{2,1,0:T(8,128)S(1)}) custom-call(s32[1]{0:T(128)} %bitcast.wall_ref, s32[1]{0:T(128)S(6)} %copy.7.steps_ref, s32[4,1,96]{2,1,0:T(1,128)S(1)} %reshape.11.mirror_ref, bf16[2,384,1152]{2,1,0:T(8,128)(2,1)S(1)} %get-tuple-element.31.ops_ref, ...), custom_call_target="tpu_custom_call" | custom-call | flops 4000000000 | bytes 4194304 | tf_op jit(solution)/shard_map/adjoint/pallas_call | solution.py:189
  22.6 4.4 %collective-permute-done.2.rest_0_ = f32[3,96,128]{2,1,0:T(8,128)S(1)} collective-permute-done((f32[3,96,128]{2,1,0:T(8,128)S(1)}, f32[3,96,128]{2,1,0:T(8,128)S(1)}, u32[]{:S(2)}, u32[]{:S(2)}) %collective-permute-start.2) | collective-permute-done | bytes 147488 | tf_op jit(solution)/shard_map/ppermute | solution.py:152
  27.0 0.0 collective-permute-start.6
  27.0 1.4 %collective-permute-start.8 = (f32[3,96,128]{2,1,0:T(8,128)S(1)}, f32[3,96,128]{2,1,0:T(8,128)S(1)}, u32[]{:S(2)}, u32[]{:S(2)}) collective-permute-start(f32[3,96,128]{2,1,0:T(8,128)S(1)} %get-tuple-element.37), channel_id=1, source_target_pairs={{0,2},{1,3},{2,0},{3,1},{4,6},{5,7},{6,4},{7,5},{8,10},{9,11},{10,... | collective-permute-start | bytes 442376 | tf_op jit(solution)/shard_map/ppermute | solution.py:152
  28.5 0.0 collective-permute-start.9
  28.5 0.4 %collective-permute-done.3.rest_1_ = f32[3,96,128]{2,1,0:T(8,128)S(1)} collective-permute-done((f32[3,96,128]{2,1,0:T(8,128)S(1)}, f32[3,96,128]{2,1,0:T(8,128)S(1)}, u32[]{:S(2)}, u32[]{:S(2)}) %collective-permute-start.3) | collective-permute-done | bytes 147488 | tf_op jit(solution)/shard_map/ppermute | solution.py:152
  28.9 1.1 %collective-permute-start.10 = (f32[3,96,128]{2,1,0:T(8,128)S(1)}, f32[3,96,128]{2,1,0:T(8,128)S(1)}, u32[]{:S(2)}, u32[]{:S(2)}) collective-permute-start(f32[3,96,128]{2,1,0:T(8,128)S(1)} %get-tuple-element.39), channel_id=1, source_target_pairs={{0,1},{1,0},{2,3},{3,2},{4,5},{5,4},{6,7},{7,6},{8,9},{9,8},{10,11... | collective-permute-start | bytes 442376 | tf_op jit(solution)/shard_map/ppermute | solution.py:152
  30.0 2.2 %collective-permute-done.5.rest_2_ = f32[3,96,128]{2,1,0:T(8,128)S(1)} collective-permute-done((f32[3,96,128]{2,1,0:T(8,128)S(1)}, f32[3,96,128]{2,1,0:T(8,128)S(1)}, u32[]{:S(2)}, u32[]{:S(2)}) %collective-permute-start.5) | collective-permute-done | bytes 147488 | tf_op jit(solution)/shard_map/ppermute | solution.py:152
  32.3 3.2 %collective-permute-done.6.rest_3_ = f32[3,96,128]{2,1,0:T(8,128)S(1)} collective-permute-done((f32[3,96,128]{2,1,0:T(8,128)S(1)}, f32[3,96,128]{2,1,0:T(8,128)S(1)}, u32[]{:S(2)}, u32[]{:S(2)}) %collective-permute-start.6) | collective-permute-done | bytes 147488 | tf_op jit(solution)/shard_map/ppermute | solution.py:152
  35.4 0.0 copy-done
  35.4 0.1 offset.1.offset_ref
  35.5 0.0 collective-permute-done.8.rest_0_
  35.5 0.0 collective-permute-done.9.rest_1_
  35.5 0.0 collective-permute-done.10.rest_2_
  35.6 0.9 %combine.1 = f32[3,96,512]{2,1,0:T(8,128)} custom-call(s32[1]{0:T(128)} %bitcast.wall_ref, f32[3,96,512]{2,1,0:T(8,128)S(1)} %offset.1.offset_ref, f32[3,96,128]{2,1,0:T(8,128)S(1)} %collective-permute-done.8.rest_0_, f32[3,96,128]{2,1,0:T(8,128)S(1)} %collective-permute-done.9.rest_1_, f32[3,96,128]{2,1,0:T(8,128)S(1)} %collective-permute-done.10.rest_2_, ...), custom_call_target="tpu_custom_call" | custom-call | flops 1000000 | bytes 3145728 | tf_op jit(solution)/shard_map/combine/pallas_call | solution.py:211
Async XLA Ops:
  0.0 14.7 %copy-start.1 = (f32[2,384,384]{2,1,0:T(8,128)S(1)}, f32[2,384,384]{2,1,0:T(8,128)}, u32[]{:S(2)}) copy-start(f32[2,384,384]{2,1,0:T(8,128)} %ops_ref) | copy-start | bytes 3538948
  1.3 10.3 %collective-permute-start = (f32[3,96,128]{2,1,0:T(8,128)S(1)}, f32[3,96,128]{2,1,0:T(8,128)S(1)}, u32[]{:S(2)}, u32[]{:S(2)}) collective-permute-start(f32[3,96,128]{2,1,0:T(8,128)S(1)} %get-tuple-element.43), channel_id=1, source_target_pairs={{0,28},{1,29},{2,30},{3,31},{4,0},{5,1},{6,2},{7,3},{8,4},{9,5},{1... | collective-permute-start | bytes 442376 | tf_op jit(solution)/shard_map/ppermute | solution.py:152
  7.3 7.4 %collective-permute-start.1 = (f32[3,96,128]{2,1,0:T(8,128)S(1)}, f32[3,96,128]{2,1,0:T(8,128)S(1)}, u32[]{:S(2)}, u32[]{:S(2)}) collective-permute-start(f32[3,96,128]{2,1,0:T(8,128)S(1)} %get-tuple-element.42), channel_id=1, source_target_pairs={{0,29},{1,28},{2,31},{3,30},{4,1},{5,0},{6,3},{7,2},{8,5},{9,4},{1... | collective-permute-start | bytes 442376 | tf_op jit(solution)/shard_map/ppermute | solution.py:152
  7.3 11.6 %collective-permute-start.4 = (f32[3,96,128]{2,1,0:T(8,128)S(1)}, f32[3,96,128]{2,1,0:T(8,128)S(1)}, u32[]{:S(2)}, u32[]{:S(2)}) collective-permute-start(f32[3,96,128]{2,1,0:T(8,128)S(1)} %get-tuple-element.44), channel_id=1, source_target_pairs={{0,30},{1,31},{2,28},{3,29},{4,2},{5,3},{6,0},{7,1},{8,6},{9,7},{1... | collective-permute-start | bytes 442376 | tf_op jit(solution)/shard_map/ppermute | solution.py:152
  9.3 11.1 %collective-permute-start.7 = (f32[3,96,128]{2,1,0:T(8,128)S(1)}, f32[3,96,128]{2,1,0:T(8,128)S(1)}, u32[]{:S(2)}, u32[]{:S(2)}) collective-permute-start(f32[3,96,128]{2,1,0:T(8,128)S(1)} %get-tuple-element.41), channel_id=1, source_target_pairs={{0,31},{1,30},{2,29},{3,28},{4,3},{5,2},{6,1},{7,0},{8,7},{9,6},{1... | collective-permute-start | bytes 442376 | tf_op jit(solution)/shard_map/ppermute | solution.py:152
  14.7 1.1 %copy-start.2 = (f32[1,3,384,128]{3,2,1,0:T(8,128)S(1)}, f32[1,3,384,128]{3,2,1,0:T(8,128)}, u32[]{:S(2)}) copy-start(f32[1,3,384,128]{3,2,1,0:T(8,128)} %param.7) | copy-start | bytes 1769476
  15.8 1.1 %copy-start.3 = (f32[1,3,384,128]{3,2,1,0:T(8,128)S(1)}, f32[1,3,384,128]{3,2,1,0:T(8,128)}, u32[]{:S(2)}) copy-start(f32[1,3,384,128]{3,2,1,0:T(8,128)} %param.8) | copy-start | bytes 1769476
  17.6 9.4 %collective-permute-start.2 = (f32[3,96,128]{2,1,0:T(8,128)S(1)}, f32[3,96,128]{2,1,0:T(8,128)S(1)}, u32[]{:S(2)}, u32[]{:S(2)}) collective-permute-start(f32[3,96,128]{2,1,0:T(8,128)S(1)} %get-tuple-element.25), channel_id=1, source_target_pairs={{0,7},{1,6},{2,5},{3,4},{4,11},{5,10},{6,9},{7,8},{8,15},{9,14},{1... | collective-permute-start | bytes 442376 | tf_op jit(solution)/shard_map/ppermute | solution.py:152
  18.5 10.4 %collective-permute-start.3 = (f32[3,96,128]{2,1,0:T(8,128)S(1)}, f32[3,96,128]{2,1,0:T(8,128)S(1)}, u32[]{:S(2)}, u32[]{:S(2)}) collective-permute-start(f32[3,96,128]{2,1,0:T(8,128)S(1)} %get-tuple-element.27), channel_id=1, source_target_pairs={{0,6},{1,7},{2,4},{3,5},{4,10},{5,11},{6,8},{7,9},{8,14},{9,15},{1... | collective-permute-start | bytes 442376 | tf_op jit(solution)/shard_map/ppermute | solution.py:152
  19.0 13.3 %collective-permute-start.5 = (f32[3,96,128]{2,1,0:T(8,128)S(1)}, f32[3,96,128]{2,1,0:T(8,128)S(1)}, u32[]{:S(2)}, u32[]{:S(2)}) collective-permute-start(f32[3,96,128]{2,1,0:T(8,128)S(1)} %get-tuple-element.29), channel_id=1, source_target_pairs={{0,5},{1,4},{2,7},{3,6},{4,9},{5,8},{6,11},{7,10},{8,13},{9,12},{1... | collective-permute-start | bytes 442376 | tf_op jit(solution)/shard_map/ppermute | solution.py:152
  20.5 15.0 %copy-start = (f32[1,3,96,512]{3,2,1,0:T(8,128)S(1)}, f32[1,3,96,512]{3,2,1,0:T(8,128)}, u32[]{:S(2)}) copy-start(f32[1,3,96,512]{3,2,1,0:T(8,128)} %param.6) | copy-start | bytes 1769476
  27.0 8.4 %collective-permute-start.6 = (f32[3,96,128]{2,1,0:T(8,128)S(1)}, f32[3,96,128]{2,1,0:T(8,128)S(1)}, u32[]{:S(2)}, u32[]{:S(2)}) collective-permute-start(f32[3,96,128]{2,1,0:T(8,128)S(1)} %get-tuple-element.30), channel_id=1, source_target_pairs={{0,4},{1,5},{2,6},{3,7},{4,8},{5,9},{6,10},{7,11},{8,12},{9,13},{1... | collective-permute-start | bytes 442376 | tf_op jit(solution)/shard_map/ppermute | solution.py:152
  27.0 8.5 %collective-permute-start.8 = (f32[3,96,128]{2,1,0:T(8,128)S(1)}, f32[3,96,128]{2,1,0:T(8,128)S(1)}, u32[]{:S(2)}, u32[]{:S(2)}) collective-permute-start(f32[3,96,128]{2,1,0:T(8,128)S(1)} %get-tuple-element.37), channel_id=1, source_target_pairs={{0,2},{1,3},{2,0},{3,1},{4,6},{5,7},{6,4},{7,5},{8,10},{9,11},{10,... | collective-permute-start | bytes 442376 | tf_op jit(solution)/shard_map/ppermute | solution.py:152
  28.5 7.1 %collective-permute-start.9 = (f32[3,96,128]{2,1,0:T(8,128)S(1)}, f32[3,96,128]{2,1,0:T(8,128)S(1)}, u32[]{:S(2)}, u32[]{:S(2)}) collective-permute-start(f32[3,96,128]{2,1,0:T(8,128)S(1)} %get-tuple-element.38), channel_id=1, source_target_pairs={{0,3},{1,2},{2,1},{3,0},{4,7},{5,6},{6,5},{7,4},{8,11},{9,10},{10,... | collective-permute-start | bytes 442376 | tf_op jit(solution)/shard_map/ppermute | solution.py:152
  28.9 6.7 %collective-permute-start.10 = (f32[3,96,128]{2,1,0:T(8,128)S(1)}, f32[3,96,128]{2,1,0:T(8,128)S(1)}, u32[]{:S(2)}, u32[]{:S(2)}) collective-permute-start(f32[3,96,128]{2,1,0:T(8,128)S(1)} %get-tuple-element.39), channel_id=1, source_target_pairs={{0,1},{1,0},{2,3},{3,2},{4,5},{5,4},{6,7},{7,6},{8,9},{9,8},{10,11... | collective-permute-start | bytes 442376 | tf_op jit(solution)/shard_map/ppermute | solution.py:152
